TPU v7x, 256 devices: a whole 4x4x8 slice. The times are simulated.
256 devices in a mesh: seq: 32 (over z_hi, x, core), head: 8 (over z_lo, y).
Axes of the slice: x: 4, y: 4, z: 8 (z_hi: 4, z_lo: 2; z = z_hi * 2 + z_lo), core: 2. Of those that a mesh axis runs over, the one named last changes fastest.
Arguments:
- query_src: bfloat16 [8192, 5120], P(('seq', 'head')), may hold values from -18 to 18
- key_src: bfloat16 [8192, 5120], P(('seq', 'head')), may hold values from -9 to 9
- value_src: bfloat16 [8192, 5120], P(('seq', 'head')), may hold values from -6 to 6
- value_edit: bfloat16 [8192, 5120], P(('seq', 'head')), may hold values from -6 to 6
- tile_mask: int32 [128, 128], P('seq'), may hold values from 0 to 1, as said below
- word_map: int32 [8192], P(('seq', 'head')), may hold values from 0 to 511
- blend_table: float32 [512, 40], replicated, may hold values from 0.1 to 0.9
Outputs:
- edited: bfloat16 [8192, 5120], P(('seq', 'head'))
Inputs may be any that keep to these rules, and one draw needn't show every extreme that they name: `tile_mask`: every diagonal entry is 1.
All inputs are finite; a program needn't handle non-finite values.
Results may differ from a plain program's by a relative error of at most 0.012.
Values may be sent and summed in bfloat16 or wider, within the bound.
A program may use at most 128 MiB of HBM per device.

v0:
```python
import jax
import jax.numpy as jnp
from jax import lax
from jax.sharding import PartitionSpec as P

TILE = 64


def on_device(query_src, key_src, value_src, value_edit, tile_mask, word_map, blend_table):
    head_total = blend_table.shape[1]
    head_size = query_src.shape[1] // head_total
    rows_in = query_src.shape[0]

    def split_heads(array):
        return array.reshape(rows_in, head_total, head_size)

    both_values = jnp.concatenate([split_heads(value_src), split_heads(value_edit)], axis=2)
    queries, key_rows, value_rows = (
        lax.all_to_all(split_heads(query_src), "head", split_axis=1, concat_axis=0, tiled=True),
        lax.all_to_all(split_heads(key_src), "head", split_axis=1, concat_axis=0, tiled=True),
        lax.all_to_all(both_values, "head", split_axis=1, concat_axis=0, tiled=True),
    )
    block_rows = queries.shape[0]
    head_count = queries.shape[1]
    tile_total = tile_mask.shape[1]
    mask_rows = tile_mask.astype(jnp.float32)
    score_scale = head_size ** (-0.5)

    def attend_rest(state, allowed_tiles, key_block, value_block):
        row_max, totals, numerators = state
        allowed = jnp.repeat(allowed_tiles, TILE, axis=0)[:, None, :]
        scores = (
            jnp.einsum("qhd,khd->qhk", queries, key_block, preferred_element_type=jnp.float32)
            * score_scale
        )
        masked = jnp.where(allowed, scores, -1e30)
        new_max = jnp.maximum(row_max, jnp.max(masked, axis=2))
        weights = jnp.where(allowed, jnp.exp(masked - new_max[:, :, None]), 0.0)
        shrink = jnp.exp(row_max - new_max)
        totals = totals * shrink + jnp.sum(weights, axis=2)
        numerators = numerators * shrink[:, :, None] + jnp.einsum(
            "qhk,khe->qhe",
            weights.astype(jnp.bfloat16),
            value_block,
            preferred_element_type=jnp.float32,
        )
        return (new_max, totals, numerators)

    def attend_block(state, key_block, value_block, first_row):
        count = key_block.shape[0]
        key_tile = (first_row + jnp.arange(count, dtype=jnp.int32)) // TILE
        onehot = (key_tile[None, :] == jnp.arange(tile_total, dtype=jnp.int32)[:, None]).astype(
            jnp.float32
        )
        allowed_tiles = jnp.dot(mask_rows, onehot) > 0.5
        return attend_rest(state, allowed_tiles, key_block, value_block)

    initial = (
        jnp.full((block_rows, head_count), -1e30, jnp.float32),
        jnp.zeros((block_rows, head_count), jnp.float32),
        jnp.zeros((block_rows, head_count, 2 * head_size), jnp.float32),
    )
    state = initial
    key_piece = lax.all_gather(key_rows, "seq", axis=0, tiled=True)
    value_piece = lax.all_gather(value_rows, "seq", axis=0, tiled=True)
    count = key_piece.shape[0]
    pieces_count = count // block_rows
    key_blocks = key_piece.reshape(pieces_count, block_rows, head_count, head_size)
    value_blocks = value_piece.reshape(pieces_count, block_rows, head_count, 2 * head_size)

    def fold_block(inner, block_item):
        key_block, value_block, block_index = block_item
        return (attend_block(inner, key_block, value_block, block_index * block_rows), None)

    state, unused = lax.scan(
        fold_block, state, (key_blocks, value_blocks, jnp.arange(pieces_count, dtype=jnp.int32))
    )
    row_max, totals, numerators = state
    results = numerators / totals[:, :, None]
    word_count = blend_table.shape[0]
    returned = lax.all_to_all(
        results.astype(jnp.bfloat16), "head", split_axis=0, concat_axis=1, tiled=True
    ).astype(results.dtype)
    word_onehot = (word_map[:, None] == jnp.arange(word_count, dtype=jnp.int32)[None, :]).astype(
        jnp.float32
    )
    mixing = jnp.dot(word_onehot, blend_table, precision=lax.Precision.HIGHEST)[:, :, None]
    mixed = mixing * returned[:, :, head_size:] + (1.0 - mixing) * returned[:, :, :head_size]
    return mixed.astype(jnp.bfloat16).reshape(rows_in, head_total * head_size)


def solution(mesh):
    return jax.shard_map(
        on_device,
        mesh=mesh,
        in_specs=(
            P(("seq", "head"), None),
            P(("seq", "head"), None),
            P(("seq", "head"), None),
            P(("seq", "head"), None),
            P("seq", None),
            P(("seq", "head")),
            P(),
        ),
        out_specs=P(("seq", "head"), None),
        check_vma=False,
    )
```

profile of v0, /device:TPU:56, one launch (start us, length us, event | category | flops | bytes accessed | tf_op | source)
XLA Modules:
  0.0 452.2 jit_solution(2481158838937249688)
XLA Ops:
  7.6 10.8 %all_to_all.63 = bf16[32,40,128]{2,0,1:T(8,128)(2,1)S(1)} all-to-all(bf16[32,40,128]{2,0,1:T(8,128)(2,1)S(1)} %copy_bitcast_fusion.2), channel_id=1, replica_groups=mesh['seq'=32,'head'=8] {'head'}, dimensions={1} | all-to-all | bytes 655360 | tf_op jit(solution)/shard_map/all_to_all | solution.py:20
  19.6 13.2 %all_to_all.64 = bf16[32,40,256]{2,0,1:T(8,128)(2,1)S(1)} all-to-all(bf16[32,40,256]{2,0,1:T(8,128)(2,1)S(1)} %copy.43), channel_id=1, replica_groups=mesh['seq'=32,'head'=8] {'head'}, dimensions={1} | all-to-all | bytes 1310720 | tf_op jit(solution)/shard_map/all_to_all | solution.py:21
  34.7 6.1 %all-to-all-start.1 = ((bf16[32,40,128]{2,0,1:T(8,128)(2,1)}), bf16[32,40,128]{2,0,1:T(8,128)(2,1)S(1)}, u32[]{:S(2)}, u32[]{:S(2)}) async-start(bf16[32,40,128]{2,0,1:T(8,128)(2,1)} %copy_bitcast_fusion.1), calls=%async_computation.1 | async-start | bytes 655360 | tf_op jit(solution)/shard_map/all_to_all | solution.py:19
  40.8 9.0 %all-to-all-done.1 = bf16[32,40,128]{2,0,1:T(8,128)(2,1)S(1)} async-done(((bf16[32,40,128]{2,0,1:T(8,128)(2,1)}), bf16[32,40,128]{2,0,1:T(8,128)(2,1)S(1)}, u32[]{:S(2)}, u32[]{:S(2)}) %all-to-all-start.1) | async-done | bytes 327712 | tf_op jit(solution)/shard_map/all_to_all | solution.py:19
  49.8 61.1 %all-gather.3.cloned.1.call-done = bf16[8192,5,128]{2,0,1:T(8,128)(2,1)} async-done(((bf16[256,5,128]{2,0,1:T(8,128)(2,1)}), bf16[8192,5,128]{2,0,1:T(8,128)(2,1)}) %all-gather.3.cloned.1.call-update) | async-done | bytes 10485776 | tf_op jit(solution)/shard_map/all_gather | solution.py:64
  110.9 140.1 %all-gather.5.cloned.1.call-done = bf16[8192,5,256]{2,0,1:T(8,128)(2,1)} async-done(((bf16[256,5,256]{2,0,1:T(8,128)(2,1)}), bf16[8192,5,256]{2,0,1:T(8,128)(2,1)}) %all-gather.5.cloned.1.call-update) | async-done | bytes 20971536 | tf_op jit(solution)/shard_map/all_gather | solution.py:65
  251.0 168.5 %while.17 = (s32[]{:T(128)}, f32[256,5]{0,1:T(8,128)S(1)}, f32[256,5]{0,1:T(8,128)S(1)}, f32[256,5,256]{0,2,1:T(8,128)S(1)}, s32[32]{0:T(128)S(1)}, /*index=5*/b...) while((s32[]{:T(128)}, f32[256,5]{0,1:T(8,128)S(1)}, ...), condition=%wide.region_3.4_spmd.clone, body=%wide.region_0.3_spmd.clone.sunk | while | flops 255896832 | bytes 8345757 | solution.py:75
  254.3 2.0 fusion.48
  259.5 2.0 fusion.48
  264.8 2.0 fusion.48
  270.1 2.0 fusion.48
  275.3 2.0 fusion.48
  280.6 2.0 fusion.48
  285.9 2.0 fusion.48
  291.1 2.0 fusion.48
  296.4 2.0 fusion.48
  301.7 2.0 fusion.48
  328.0 2.0 fusion.48
  343.8 2.0 fusion.48
  391.2 2.0 fusion.48
  407.0 2.0 fusion.48
  421.6 2.9 divide_convert_fusion
  424.6 5.8 %all-to-all-start.3 = ((bf16[256,5,256]{2,1,0:T(8,128)(2,1)}), bf16[256,5,256]{2,1,0:T(8,128)(2,1)S(1)}, u32[]{:S(2)}, u32[]{:S(2)}) async-start(bf16[256,5,256]{2,1,0:T(8,128)(2,1)} %divide_convert_fusion), calls=%async_computation.3 | async-start | bytes 2097152 | tf_op jit(solution)/shard_map/all_to_all | solution.py:81
  430.7 13.1 %all-to-all-done.3 = bf16[256,5,256]{2,1,0:T(8,128)(2,1)S(1)} async-done(((bf16[256,5,256]{2,1,0:T(8,128)(2,1)}), bf16[256,5,256]{2,1,0:T(8,128)(2,1)S(1)}, u32[]{:S(2)}, u32[]{:S(2)}) %all-to-all-start.3) | async-done | bytes 655392 | tf_op jit(solution)/shard_map/all_to_all | solution.py:81
  (379 shorter events, 125.3 us)
Async XLA Ops:
  6.5 1.0 copy-start
  6.5 12.7 %copy-start.1 = (bf16[32,5120]{1,0:T(8,128)(2,1)S(1)}, bf16[32,5120]{1,0:T(8,128)(2,1)}, u32[]{:S(2)}) copy-start(bf16[32,5120]{1,0:T(8,128)(2,1)} %param.11) | copy-start | bytes 983044
  6.5 104.4 %all-gather.3.cloned.1.call-start = ((), (), s32[]{:S(2)}) async-start(), calls=%async_computation.4 | async-start | bytes 10813440 | tf_op jit(solution)/shard_map/all_gather | solution.py:64
  7.6 11.7 %copy-start.2 = (bf16[32,5120]{1,0:T(8,128)(2,1)S(1)}, bf16[32,5120]{1,0:T(8,128)(2,1)}, u32[]{:S(2)}) copy-start(bf16[32,5120]{1,0:T(8,128)(2,1)} %param.12) | copy-start | bytes 983044
  19.2 231.8 %all-gather.5.cloned.1.call-start = ((), (), s32[]{:S(2)}) async-start(), calls=%async_computation.5 | async-start | bytes 21626880 | tf_op jit(solution)/shard_map/all_gather | solution.py:65
  32.8 1.1 copy-start.3
  33.7 7.1 %copy-start.5 = (s32[4,128]{1,0:T(4,128)S(1)}, s32[4,128]{1,0:T(4,128)}, u32[]{:S(2)}) copy-start(s32[4,128]{1,0:T(4,128)} %param.13) | copy-start | bytes 6148
  34.7 15.1 %all-to-all-start.1 = ((bf16[32,40,128]{2,0,1:T(8,128)(2,1)}), bf16[32,40,128]{2,0,1:T(8,128)(2,1)S(1)}, u32[]{:S(2)}, u32[]{:S(2)}) async-start(bf16[32,40,128]{2,0,1:T(8,128)(2,1)} %copy_bitcast_fusion.1), calls=%async_computation.1 | async-start | bytes 655360 | tf_op jit(solution)/shard_map/all_to_all | solution.py:19
  424.6 5.8 %copy-start.4 = (f32[512,40]{0,1:T(8,128)S(1)}, f32[512,40]{0,1:T(8,128)}, u32[]{:S(2)}) copy-start(f32[512,40]{0,1:T(8,128)} %param.15) | copy-start | bytes 245764
  424.6 5.8 %copy-start.6 = (s32[32]{0:T(128)S(1)}, s32[32]{0:T(128)}, u32[]{:S(2)}) copy-start(s32[32]{0:T(128)} %param.14) | copy-start | bytes 388
  424.6 19.2 %all-to-all-start.3 = ((bf16[256,5,256]{2,1,0:T(8,128)(2,1)}), bf16[256,5,256]{2,1,0:T(8,128)(2,1)S(1)}, u32[]{:S(2)}, u32[]{:S(2)}) async-start(bf16[256,5,256]{2,1,0:T(8,128)(2,1)} %divide_convert_fusion), calls=%async_computation.3 | async-start | bytes 2097152 | tf_op jit(solution)/shard_map/all_to_all | solution.py:81
Sparse Core Ops, SparseCore 0:
  19.3 91.5 all-gather.2
  113.5 137.4 all-gather.4
where the time goes:
time: 458 us; the launch traced here: 452 us
  waiting for transfers between devices  223 us (49%)
  matrix products  112 us (24%)
  local copies, waits for them, and re-layouts  31.4 us (7%)
  blocking collectives  24.1 us (5%)
  loops' own time  23.3 us (5%)
  between operations  13.5 us (3%)
  other arithmetic  13 us (3%)
  starting transfers between devices  11.9 us (3%)
    all_gather x1, waiting for transfers between devices, on_device(): value_piece = lax.all_gather(value_rows, 'seq', axis=0, tiled=True)  140 us
    dot_general x32, matrix products, attend_rest(): jnp.einsum('qhk,khe->qhe', weights.astype(jnp.bfloat16), value_block, pre...  63.8 us
    all_gather x1, waiting for transfers between devices, on_device(): key_piece = lax.all_gather(key_rows, 'seq', axis=0, tiled=True)  61.1 us
    dot_general x32, matrix products, attend_rest(): jnp.einsum('qhd,khd->qhk', queries, key_block, preferred_element_type=jnp...  43 us
    another operation x1, loops' own time, on_device(): lax.scan(fold_block, state, (key_blocks, value_blocks, jnp.arange(pieces_...  23.3 us
    dynamic_slice x32, local copies, waits for them, and re-layouts, on_device(): lax.scan(fold_block, state, (key_blocks, value_blocks, jnp.arange(pieces_...  18.8 us
    all_to_all x1, blocking collectives, on_device(): lax.all_to_all(both_values, 'head', split_axis=1, concat_axis=0, tiled=True)  13.2 us
    all_to_all x1, waiting for transfers between devices, on_device(): lax.all_to_all(results.astype(jnp.bfloat16), 'head', split_axis=0, concat...  13.1 us
  transfers between devices with their start and end apart: 4, of which 4 were waited for; matrix products, arithmetic and copies ran while one was open for 1% of the time, Pallas kernels for 0%

commit v1 on v0

v1 whole, which is shorter than its diff:
```python
import jax
import jax.numpy as jnp
from jax import lax
from jax.experimental import pallas as pl
from jax.experimental.pallas import tpu as pltpu
from jax.sharding import PartitionSpec as P

MESH = pl.DeviceIdType.MESH
HD = 128
NX, NY, NZ, NC = 4, 4, 8, 2
HZ = 5
TB = 32
SLOTS = 11
ROWS = SLOTS * 4 * TB
CK = 1024
QC = 352
MASKED = -(2.0**100)
OFFS = (0, 1, -1, 2, -2, 3, -3, 4)
LOG2E = 1.4426950408889634


def offset_of(s):
    half = (s + 1) // 2
    return half * (2 * (s % 2) - 1)


def copy_wait(ref, sem):
    pltpu.make_async_copy(ref, ref, sem).wait()


def body(
    q_ref, k_ref, v_ref, w_ref, ext_ref, out_ref,
    zq, zx, zkv, hq, hx, hk, qb, xb, kv, oh, qa, mix, mm, ll, oo, ro, ox,
    zq_s, zq_r, zx_s, zx_r, zk_s, zk_r,
    pq_s, pq_r, pqe_r, px_s, px_r, pxe_r, bq_s, bq_r, bx_s, bx_r,
    p1_s, p1_r, p1e_r, p2_s, p2e_s, p2_r, c_s, c_r,
    r1_s, r1_r, rb_s, rb_r, re_s, re_r, r2_s, r2_r,
):
    seq = lax.axis_index("seq")
    head = lax.axis_index("head")
    z = (seq // 8) * 2 + head // 4
    x = (seq // 2) % 4
    c = seq % 2
    y = head % 4
    last = y == 3

    def dev(dx, dy, dz, dc):
        return ((dz // 2) * 8 + dx * 2 + dc, (dz % 2) * 4 + dy)

    def send(src, dst, ss, rs, to):
        pltpu.make_async_remote_copy(
            src_ref=src, dst_ref=dst, send_sem=ss, recv_sem=rs, device_id=to, device_id_type=MESH
        ).start()

    def local(src, dst, rs):
        pltpu.make_async_copy(src, dst, rs).start()

    def wait_send(src, ss):
        copy_wait(src, ss)

    def cols(ref3, zz, count):
        return ref3.at[:, pl.ds(pl.multiple_of(zz * (HZ * HD), HD), count * HD)]

    def lanes(j):
        return pl.ds(pl.multiple_of(j * HD, HD), HD)

    def block(i):
        return pl.ds(pl.multiple_of(i * TB, TB), TB)

    barrier = pltpu.get_barrier_semaphore()
    for d in range(1, NZ):
        pl.semaphore_signal(barrier, inc=1, device_id=dev(x, y, (z + d) % NZ, c), device_id_type=MESH)
    for d in range(1, NX * NY):
        pl.semaphore_signal(
            barrier, inc=1, device_id=dev((x + d // 4) % 4, (y + d % 4) % 4, z, c), device_id_type=MESH
        )
    pl.semaphore_signal(barrier, inc=1, device_id=dev(x, y, z, 1 - c), device_id_type=MESH)
    pl.semaphore_wait(barrier, NZ + NX * NY - 1)

    local(cols(q_ref, z, HZ), zq.at[z], zq_r.at[z])
    local(ext_ref.at[z], zx.at[z], zx_r.at[z])
    for s in range(1, NZ):
        to = (z - OFFS[s] + NZ) % NZ
        send(cols(q_ref, to, HZ), zq.at[z], zq_s.at[s], zq_r.at[z], dev(x, y, to, c))
        send(ext_ref.at[to], zx.at[z], zx_s.at[s], zx_r.at[z], dev(x, y, to, c))
    for i, ref in enumerate((k_ref, v_ref, w_ref)):
        local(cols(ref, z, HZ), zkv.at[z, i], zk_r.at[z])
    for s in range(1, NZ):
        to = (z - OFFS[s] + NZ) % NZ
        for i, ref in enumerate((k_ref, v_ref, w_ref)):
            send(cols(ref, to, HZ), zkv.at[z, i], zk_s.at[s], zk_r.at[z], dev(x, y, to, c))

    row = lax.broadcasted_iota(jnp.int32, (CK, HD), 0)
    lane = lax.broadcasted_iota(jnp.int32, (CK, HD), 1)
    from_line, inner = (row // 128) % 4, (row // TB) % 4
    row_x = jnp.where(last, from_line, inner)
    row_y = jnp.where(last, inner, from_line)
    tile = row_x * 8 + (row // 512) * 4 + row_y // 2

    def fill_onehot(zz, carry):
        base = (zz // 2) * 32 + (zz % 2) * 2
        oh[zz] = jnp.where(lane - base == tile, 1.0, 0.0).astype(jnp.bfloat16)
        return carry

    lax.fori_loop(0, NZ, fill_onehot, 0)
    mm[...] = jnp.full(mm.shape, MASKED, jnp.float32)
    ll[...] = jnp.zeros(ll.shape, jnp.float32)

    def clear(i, carry):
        oo[pl.ds(pl.multiple_of(i * 128, 128), 128), :] = jnp.zeros((128, 2 * HD), jnp.float32)
        return carry

    lax.fori_loop(0, SLOTS, clear, 0)

    @pl.when(y >= 2)
    def _():
        qb[10] = jnp.zeros(qb.shape[1:], qb.dtype)
        xb[10] = jnp.zeros(xb.shape[1:], xb.dtype)

    @pl.when(last)
    def _():
        qb[8:10] = jnp.zeros((2,) + qb.shape[1:], qb.dtype)
        xb[8:10] = jnp.zeros((2,) + xb.shape[1:], xb.dtype)

    def spread_queries():
        for i in range(NZ):
            copy_wait(zq.at[i], zq_r.at[i])
            copy_wait(zx.at[i], zx_r.at[i])

        def to_lines(qdst, xdst):
            local(zq.at[:, :, lanes(x)], qdst, pq_r.at[x])
            local(zx, xdst, px_r.at[x])
            for d in range(1, 4):
                j = (x + d) % 4
                send(zq.at[:, :, lanes(j)], qdst, pq_s.at[d], pq_r.at[x], dev(j, y, z, c))
                send(zx, xdst, px_s.at[d], px_r.at[x], dev(j, y, z, c))

        @pl.when(last)
        def _():
            to_lines(hq.at[:, block(x), :], hx.at[:, x])
            local(zq.at[:, :, pl.ds(4 * HD, HD)], qb.at[pl.ds(0, 8), pl.ds(3 * TB, TB), :], pqe_r.at[3])
            local(zx, xb.at[pl.ds(0, 8), 3], pxe_r.at[3])

        @pl.when(jnp.logical_not(last))
        def _():
            to_lines(qb.at[pl.ds(0, 8), block(x), :], xb.at[pl.ds(0, 8), x])
            send(
                zq.at[:, :, pl.ds(4 * HD, HD)], qb.at[pl.ds(0, 8), block(y), :],
                pq_s.at[0], pqe_r.at[y], dev(x, 3, z, c),
            )
            send(zx, xb.at[pl.ds(0, 8), y], px_s.at[0], pxe_r.at[y], dev(x, 3, z, c))

    def lend_queries():
        for i in range(4):
            copy_wait(hq.at[:, pl.ds(0, TB), :], pq_r.at[i])
            copy_wait(zx, px_r.at[i])

        @pl.when(last)
        def _():
            for t in range(3):
                n = 3 if t < 2 else 2
                send(hq.at[pl.ds(3 * t, n)], qb.at[pl.ds(8, n)], bq_s.at[t], bq_r, dev(x, t, z, c))
                send(hx.at[pl.ds(3 * t, n)], xb.at[pl.ds(8, n)], bx_s.at[t], bx_r, dev(x, t, z, c))
            for i in range(4):
                copy_wait(hq.at[:, pl.ds(0, TB), :], pqe_r.at[i])
                copy_wait(zx, pxe_r.at[i])

    def ready_queries():
        @pl.when(y < 2)
        def _():
            copy_wait(qb.at[pl.ds(8, 3)], bq_r)
            copy_wait(xb.at[pl.ds(8, 3)], bx_r)

        @pl.when(y == 2)
        def _():
            copy_wait(qb.at[pl.ds(8, 2)], bq_r)
            copy_wait(xb.at[pl.ds(8, 2)], bx_r)

        which = 1 + jnp.where(last, 4, x)
        sub = lax.broadcasted_iota(jnp.int32, (4, 8, 128), 1)
        diag = lax.broadcasted_iota(jnp.int32, (4, TB, 128), 1) == lax.broadcasted_iota(
            jnp.int32, (4, TB, 128), 2
        )

        def one(i, carry):
            rows = pl.ds(pl.multiple_of(i * 128, 128), 128)
            extra = xb[i]
            qa[rows, 0:HD] = qb[i]
            bias = jnp.broadcast_to(extra[:, 0:1, :], (4, TB, 128))
            qa[rows, HD : 2 * HD] = bias.reshape(128, 128).astype(jnp.bfloat16)
            shares = jnp.sum(jnp.where(sub == which, extra, 0.0), axis=1, keepdims=True)
            column = jnp.sum(jnp.where(diag, shares, 0.0), axis=2, keepdims=True)
            mix[rows, :] = jnp.broadcast_to(column, (4, TB, 128)).reshape(128, 128)
            return carry

        lax.fori_loop(0, SLOTS, one, 0)

    def source(s):
        return (z + offset_of(s) + NZ) % NZ

    def stage_one(s):
        zz = source(s)
        copy_wait(zkv.at[zz], zk_r.at[zz])

        def to_lines(dst):
            local(zkv.at[zz, :, :, lanes(x)], dst, p1_r.at[s, x])
            for d in range(1, 4):
                j = (x + d) % 4
                send(zkv.at[zz, :, :, lanes(j)], dst, p1_s.at[s, d], p1_r.at[s, x], dev(j, y, z, c))

        @pl.when(last)
        def _():
            to_lines(hk.at[zz, :, block(x), :])
            local(
                zkv.at[zz, :, :, pl.ds(4 * HD, HD)], kv.at[zz, :, c, x, pl.ds(3 * TB, TB), :], p1e_r.at[s, 3]
            )

        @pl.when(jnp.logical_not(last))
        def _():
            to_lines(kv.at[zz, :, c, y, block(x), :])
            send(
                zkv.at[zz, :, :, pl.ds(4 * HD, HD)], kv.at[zz, :, c, x, block(y), :],
                p1_s.at[s, 0], p1e_r.at[s, y], dev(x, 3, z, c),
            )

    def stage_two(s):
        zz = source(s)
        piece = hk.at[zz, :, pl.ds(0, TB), :]
        for i in range(4):
            copy_wait(piece, p1_r.at[s, i])

        @pl.when(last)
        def _():
            for t in range(3):
                send(hk.at[zz], kv.at[zz, :, c, 3], p2_s.at[s, t], p2_r.at[s, 3], dev(x, t, z, c))
            for i in range(4):
                copy_wait(piece, p1e_r.at[s, i])
            own = kv.at[zz, :, c, x]
            for d in range(1, 4):
                send(own, own, p2e_s.at[s, d], p2_r.at[s, x], dev((x + d) % 4, y, z, c))

        @pl.when(jnp.logical_not(last))
        def _():
            own = kv.at[zz, :, c, y]
            for d in range(1, 3):
                send(own, own, p2_s.at[s, d], p2_r.at[s, y], dev(x, (y + d) % 3, z, c))

    def stage_three(s):
        zz = source(s)
        own = jnp.where(last, x, y)
        for d in range(1, 4):
            copy_wait(hk.at[zz], p2_r.at[s, (own + d) % 4])
        half = kv.at[zz, :, c]
        send(half, half, c_s.at[s], c_r.at[s], dev(x, y, z, 1 - c))

    scale = HD ** (-0.5) * LOG2E

    def attend(s):
        zz = source(s)
        copy_wait(kv.at[zz, :, 0], c_r.at[s])

        def some_rows(i, carry):
            rows = pl.ds(pl.multiple_of(i * QC, 32), QC)
            keys = jnp.concatenate([kv[zz, 0].reshape(CK, HD), oh[zz]], axis=1)
            values = jnp.concatenate([kv[zz, 1].reshape(CK, HD), kv[zz, 2].reshape(CK, HD)], axis=1)
            scores = lax.dot_general(
                qa[rows, :], keys, (((1,), (1,)), ((), ())), preferred_element_type=jnp.float32
            )
            old = mm[rows, :]
            new = jnp.maximum(old, jnp.max(scores, axis=1, keepdims=True))
            weights = jnp.exp2((scores - new[:, 0:1]) * scale)
            shrink = jnp.exp2((old - new) * scale)
            part = weights[:, 0:128]
            for t in range(1, CK // 128):
                part = part + weights[:, t * 128 : (t + 1) * 128]
            mm[rows, :] = new
            ll[rows, :] = ll[rows, :] * shrink + part
            sums = jnp.dot(weights.astype(jnp.bfloat16), values, preferred_element_type=jnp.float32)
            oo[rows, :] = oo[rows, :] * jnp.concatenate([shrink, shrink], axis=1) + sums
            return carry

        lax.fori_loop(0, ROWS // QC, some_rows, 0)

    spread_queries()
    stage_one(0)
    lend_queries()
    stage_one(1)
    stage_two(0)
    ready_queries()
    stage_one(2)
    stage_two(1)
    stage_three(0)

    def step(t, carry):
        attend(t)

        @pl.when(t + 3 < NZ)
        def _():
            stage_one(t + 3)

        @pl.when(t + 2 < NZ)
        def _():
            stage_two(t + 2)

        @pl.when(t + 1 < NZ)
        def _():
            stage_three(t + 1)

        return carry

    lax.fori_loop(0, NZ, step, 0)

    def finish(i, carry):
        rows = pl.ds(pl.multiple_of(i * 128, 128), 128)
        total = jnp.sum(ll[rows, :], axis=1, keepdims=True)
        share = mix[rows, :]
        both = oo[rows, :] / total
        ro[i] = (share * both[:, HD:] + (1.0 - share) * both[:, :HD]).astype(jnp.bfloat16)
        return carry

    lax.fori_loop(0, SLOTS, finish, 0)

    @pl.when(last)
    def _():
        e_lanes = pl.ds(4 * HD, HD)
        local(ro.at[pl.ds(0, 8), pl.ds(3 * TB, TB), :], ox.at[:, :, e_lanes], re_r)
        for t in range(3):
            send(ro.at[pl.ds(0, 8), pl.ds(t * TB, TB), :], ox.at[:, :, e_lanes], r1_s.at[t], re_r, dev(x, t, z, c))
        for j in range(4):
            for t in range(3):
                n = 3 if t < 2 else 2
                copy_wait(ox.at[pl.ds(3 * t, n), :, lanes(j)], rb_r.at[j, t])

    @pl.when(jnp.logical_not(last))
    def _():
        mine = lanes(x)
        local(ro.at[pl.ds(0, 8), block(x), :], ox.at[:, :, mine], r1_r.at[x])
        for d in range(1, 4):
            j = (x + d) % 4
            send(ro.at[pl.ds(0, 8), block(j), :], ox.at[:, :, mine], r1_s.at[d], r1_r.at[x], dev(j, y, z, c))
        for i in range(4):

            @pl.when(y < 2)
            def _():
                send(
                    ro.at[pl.ds(8, 3), pl.ds(i * TB, TB), :], ox.at[pl.ds(3 * y, 3), :, mine],
                    rb_s.at[i], rb_r.at[x, y], dev(i, 3, z, c),
                )

            @pl.when(y == 2)
            def _():
                send(
                    ro.at[pl.ds(8, 2), pl.ds(i * TB, TB), :], ox.at[pl.ds(6, 2), :, mine],
                    rb_s.at[i], rb_r.at[x, 2], dev(i, 3, z, c),
                )

        for i in range(4):
            copy_wait(ox.at[:, :, lanes(i)], r1_r.at[i])

    copy_wait(ox.at[:, :, pl.ds(4 * HD, HD)], re_r)
    target = cols(out_ref, z, HZ)
    local(ox.at[z], target, r2_r.at[z])
    for s in range(1, NZ):
        to = (z - OFFS[s] + NZ) % NZ
        send(ox.at[to], target, r2_s.at[s], r2_r.at[z], dev(x, y, to, c))

    for s in range(1, NZ):
        wait_send(zq.at[0], zq_s.at[s])
        wait_send(zx.at[0], zx_s.at[s])
        wait_send(zkv.at[0], zk_s.at[s])
    for d in range(1, 4):
        wait_send(hq.at[:, pl.ds(0, TB), :], pq_s.at[d])
        wait_send(zx, px_s.at[d])

    def left(s, carry):
        for d in range(1, 4):
            wait_send(hk.at[0, :, pl.ds(0, TB), :], p1_s.at[s, d])
        wait_send(kv.at[0, :, 0], c_s.at[s])

        @pl.when(last)
        def _():
            for t in range(3):
                wait_send(hk.at[0], p2_s.at[s, t])
                wait_send(hk.at[0], p2e_s.at[s, t + 1])

        @pl.when(jnp.logical_not(last))
        def _():
            wait_send(hk.at[0, :, pl.ds(0, TB), :], p1_s.at[s, 0])
            for d in range(1, 3):
                wait_send(hk.at[0], p2_s.at[s, d])

        return carry

    lax.fori_loop(0, NZ, left, 0)

    @pl.when(last)
    def _():
        for t in range(3):
            n = 3 if t < 2 else 2
            wait_send(hq.at[pl.ds(0, n)], bq_s.at[t])
            wait_send(hx.at[pl.ds(0, n)], bx_s.at[t])
            wait_send(hq.at[:, pl.ds(0, TB), :], r1_s.at[t])

    @pl.when(jnp.logical_not(last))
    def _():
        wait_send(hq.at[:, pl.ds(0, TB), :], pq_s.at[0])
        wait_send(zx, px_s.at[0])
        for d in range(1, 4):
            wait_send(hq.at[:, pl.ds(0, TB), :], r1_s.at[d])

        @pl.when(y < 2)
        def _():
            for i in range(4):
                wait_send(hq.at[pl.ds(0, 3), pl.ds(0, TB), :], rb_s.at[i])

        @pl.when(y == 2)
        def _():
            for i in range(4):
                wait_send(hq.at[pl.ds(0, 2), pl.ds(0, TB), :], rb_s.at[i])

    for s in range(1, NZ):
        wait_send(ox.at[0], r2_s.at[s])
    for i in range(NZ):
        copy_wait(ox.at[0], r2_r.at[i])


def on_device(query_src, key_src, value_src, value_edit, tile_mask, word_map, blend_table):
    words, heads = blend_table.shape
    half = lax.axis_index("head") // 2
    mask_row = lax.dynamic_index_in_dim(tile_mask, half, 0, keepdims=False)
    bias = jnp.where(mask_row == 1, 0.0, MASKED).astype(jnp.float32)
    onehot = (jnp.arange(words, dtype=jnp.int32)[:, None] == word_map[None, :]).astype(jnp.float32)
    shares = lax.dot_general(
        blend_table, onehot, (((0,), (0,)), ((), ())), precision=lax.Precision.HIGHEST
    )
    shares = jnp.pad(shares.reshape(NZ, HZ, TB), ((0, 0), (0, 0), (0, 128 - TB)))
    ext = jnp.concatenate(
        [jnp.broadcast_to(bias, (NZ, 1, 128)), shares, jnp.zeros((NZ, 2, 128), jnp.float32)], axis=1
    )
    bf, f32 = jnp.bfloat16, jnp.float32
    dma = pltpu.SemaphoreType.DMA
    anywhere = pl.BlockSpec(memory_space=pl.ANY)
    vmem = pl.BlockSpec(memory_space=pltpu.VMEM)
    return pl.pallas_call(
        body,
        out_shape=jax.ShapeDtypeStruct(query_src.shape, bf),
        in_specs=[anywhere] * 4 + [vmem],
        out_specs=anywhere,
        scratch_shapes=[
            pltpu.VMEM((NZ, TB, HZ * HD), bf),
            pltpu.VMEM((NZ, 8, 128), f32),
            pltpu.VMEM((NZ, 3, TB, HZ * HD), bf),
            pltpu.VMEM((NZ, 128, HD), bf),
            pltpu.VMEM((NZ, 4, 8, 128), f32),
            pltpu.VMEM((NZ, 3, 128, HD), bf),
            pltpu.VMEM((SLOTS, 128, HD), bf),
            pltpu.VMEM((SLOTS, 4, 8, 128), f32),
            pltpu.VMEM((NZ, 3, NC, 4, 128, HD), bf),
            pltpu.VMEM((NZ, CK, HD), bf),
            pltpu.VMEM((ROWS, 2 * HD), bf),
            pltpu.VMEM((ROWS, 128), f32),
            pltpu.VMEM((ROWS, 128), f32),
            pltpu.VMEM((ROWS, 128), f32),
            pltpu.VMEM((ROWS, 2 * HD), f32),
            pltpu.VMEM((SLOTS, 128, HD), bf),
            pltpu.VMEM((NZ, TB, HZ * HD), bf),
            dma((NZ,)), dma((NZ,)), dma((NZ,)), dma((NZ,)), dma((NZ,)), dma((NZ,)),
            dma((4,)), dma((4,)), dma((4,)), dma((4,)), dma((4,)), dma((4,)),
            dma((3,)), dma(()), dma((3,)), dma(()),
            dma((NZ, 4)), dma((NZ, 4)), dma((NZ, 4)),
            dma((NZ, 3)), dma((NZ, 4)), dma((NZ, 4)), dma((NZ,)), dma((NZ,)),
            dma((4,)), dma((4,)), dma((4,)), dma((4, 3)), dma((1,)), dma(()),
            dma((NZ,)), dma((NZ,)),
        ],
        compiler_params=pltpu.CompilerParams(
            collective_id=0, has_side_effects=True, vmem_limit_bytes=48 * 1024 * 1024
        ),
        cost_estimate=pl.CostEstimate(
            flops=4 * ROWS * 8192 * 256, bytes_accessed=8 * 1024 * 1024, transcendentals=ROWS * 8192
        ),
    )(query_src, key_src, value_src, value_edit, ext)


def solution(mesh):
    return jax.shard_map(
        on_device,
        mesh=mesh,
        in_specs=(
            P(("seq", "head"), None),
            P(("seq", "head"), None),
            P(("seq", "head"), None),
            P(("seq", "head"), None),
            P("seq", None),
            P(("seq", "head")),
            P(),
        ),
        out_specs=P(("seq", "head"), None),
        check_vma=False,
    )
```

time: 458 us -> 117 us (0.26)
  waiting for transfers between devices: 223 us -> 0 us
  matrix products: 112 us -> 0.25 us
  Pallas kernels: 0 us -> 109 us
  local copies, waits for them, and re-layouts: 31.4 us -> 5.46 us
  blocking collectives: 24.1 us -> 0 us
  loops' own time: 23.3 us -> 0 us
  between operations: 13.5 us -> 0.03 us
  other arithmetic: 13 us -> 0.79 us
  starting transfers between devices: 11.9 us -> 0 us
    all_gather x2 -> x0, waiting for transfers between devices: 201 us -> none  [the longest x1 140 us: on_device(): value_piece = lax.all_gather(value_rows, 'seq', axis=0, tiled=True)]
    dot_general x97 -> x1, matrix products: 112 us -> 0.25 us  [on_device(): lax.dot_general(blend_table, onehot, (((0,), (0,)), ((), ())), precision=...]
    pallas_call x0 -> x1, Pallas kernels: none -> 109 us  [on_device(): pl.pallas_call(body, out_shape=jax.ShapeDtypeStruct(query_src.shape, bf),...]
    all_to_all x2 -> x0, blocking collectives: 24.1 us -> none  [the longest x1 13.2 us: on_device(): lax.all_to_all(both_values, 'head', split_axis=1, concat_axis=0, tiled=True)]
    another operation x1 -> x0, loops' own time: 23.3 us -> none  [on_device(): lax.scan(fold_block, state, (key_blocks, value_blocks, jnp.arange(pieces_...]
    all_to_all x2 -> x0, waiting for transfers between devices: 22 us -> none  [the longest x1 13.1 us: on_device(): lax.all_to_all(results.astype(jnp.bfloat16), 'head', split_axis=0, concat...]
    dynamic_slice x32 -> x0, local copies, waits for them, and re-layouts: 18.8 us -> none  [on_device(): lax.scan(fold_block, state, (key_blocks, value_blocks, jnp.arange(pieces_...]
    all_to_all x2 -> x0, starting transfers between devices: 11.8 us -> none  [the longest x1 6.09 us: on_device(): lax.all_to_all(split_heads(query_src), 'head', split_axis=1, concat_axis=...]
  transfers between devices with their start and end apart: 4 -> 0, of which waited for: 4 -> 0; matrix products, arithmetic and copies ran while one was open for 1% -> 0% of each run, Pallas kernels for 0% -> 0%
where the time goes in v1:
time: 117 us; the launch traced here: 116 us
  Pallas kernels  109 us (93%)
  local copies, waits for them, and re-layouts  5.46 us (5%)
    pallas_call x1, Pallas kernels, on_device(): pl.pallas_call(body, out_shape=jax.ShapeDtypeStruct(query_src.shape, bf),...  109 us
    unnamed x13, local copies, waits for them, and re-layouts  5.28 us

profile of v1, /device:TPU:56, one launch (start us, length us, event | category | flops | bytes accessed | tf_op | source)
XLA Modules:
  0.0 115.6 jit_solution(3353290837584937797)
XLA Ops:
  0.0 0.0 copy-start
  0.0 0.7 fusion.5
  0.7 0.1 pad.7.clone
  0.8 0.0 copy-start.5
  0.8 0.1 copy-done
  0.9 0.6 copy-done.5
  1.5 0.2 convolution_bitcast_fusion
  1.7 0.1 copy.9
  1.8 0.1 fusion.3.ext_ref
  1.9 0.0 copy-start.1
  1.9 1.0 copy-done.1
  2.9 0.0 copy-start.2
  2.9 1.0 copy-done.2
  3.9 0.0 copy-start.3
  3.9 1.0 copy-done.3
  4.8 0.0 copy-start.4
  4.8 1.0 copy-done.4
  5.8 109.0 %shard_map.73 = bf16[32,5120]{1,0:T(8,128)(2,1)S(1)} custom-call(bf16[32,5120]{1,0:T(8,128)(2,1)S(1)} %copy-done.1, bf16[32,5120]{1,0:T(8,128)(2,1)S(1)} %copy-done.2, bf16[32,5120]{1,0:T(8,128)(2,1)S(1)} %copy-done.3, bf16[32,5120]{1,0:T(8,128)(2,1)S(1)} %copy-done.4, f32[8,8,128]{2,1,0:T(8,128)S(1)} %fusion.3.ext_ref), custom_call_target="tpu_custom_call" | custom-call | flops 11811160064 | bytes 8388608 | tf_op jit(solution)/shard_map/pallas_call | solution.py:444
  114.8 0.7 copy.11
  (3 shorter events, 0.0 us)
Async XLA Ops:
  0.0 0.9 copy-start
  0.8 0.7 copy-start.5
  1.9 1.0 copy-start.1
  2.9 1.0 copy-start.2
  3.9 1.0 copy-start.3
  4.8 1.0 copy-start.4

commit v2 on v1

--- a/solution.py
+++ b/solution.py
@@ -13,9 +13,13 @@
 SLOTS = 11
 ROWS = SLOTS * 4 * TB
 CK = 1024
-QC = 352
+QC = 704
 MASKED = -(2.0**100)
 OFFS = (0, 1, -1, 2, -2, 3, -3, 4)
+VMEM_LIMIT = 60 * 1024 * 1024
+LAGS = (0, 2, 4, 6)
+READY = 8
+AHEAD = 7
 LOG2E = 1.4426950408889634
 
 
@@ -29,11 +33,11 @@
 
 
 def body(
-    q_ref, k_ref, v_ref, w_ref, ext_ref, out_ref,
-    zq, zx, zkv, hq, hx, hk, qb, xb, kv, oh, qa, mix, mm, ll, oo, ro, ox,
+    q_ref, k_ref, v_ref, w_ref, mask_ref, word_ref, blend_ref, out_ref,
+    ext_ref, zq, zx, zkv, hq, hx, hk, ek, fk, qb, xb, kv, oh, qa, mix, mm, ll, oo, ro, ox,
     zq_s, zq_r, zx_s, zx_r, zk_s, zk_r,
     pq_s, pq_r, pqe_r, px_s, px_r, pxe_r, bq_s, bq_r, bx_s, bx_r,
-    p1_s, p1_r, p1e_r, p2_s, p2e_s, p2_r, c_s, c_r,
+    p1_s, p1_r, p1e_r, p1e_s, p2_s, p2_r, e_s, e_r, f_r, p3_s, h_r, c_s, c_r,
     r1_s, r1_r, rb_s, rb_r, re_s, re_r, r2_s, r2_r,
 ):
     seq = lax.axis_index("seq")
@@ -43,6 +47,8 @@
     c = seq % 2
     y = head % 4
     last = y == 3
+    even = y % 2 == 0
+    slot = (y % 2) * 2 + y // 2
 
     def dev(dx, dy, dz, dc):
         return ((dz // 2) * 8 + dx * 2 + dc, (dz % 2) * 4 + dy)
@@ -75,6 +81,47 @@
             barrier, inc=1, device_id=dev((x + d // 4) % 4, (y + d % 4) % 4, z, c), device_id_type=MESH
         )
     pl.semaphore_signal(barrier, inc=1, device_id=dev(x, y, z, 1 - c), device_id_type=MESH)
+
+    words = blend_ref.shape[1]
+    hit = lax.broadcasted_iota(jnp.int32, (words, TB), 0) == word_ref[...]
+    shares = jnp.dot(
+        blend_ref[...], hit.astype(jnp.float32),
+        precision=lax.Precision.HIGHEST, preferred_element_type=jnp.float32,
+    )
+    mask_row = jnp.where(mask_ref[pl.ds(head // 2, 1), :] == 1, 0.0, MASKED).astype(jnp.float32)
+    for i in range(NZ):
+        ext_ref[i] = jnp.zeros((8, 128), jnp.float32)
+        ext_ref[i, 0:1, :] = mask_row
+        ext_ref[i, 1 : 1 + HZ, 0:TB] = shares[i * HZ : (i + 1) * HZ, :]
+    row = lax.broadcasted_iota(jnp.int32, (CK, HD), 0)
+    lane = lax.broadcasted_iota(jnp.int32, (CK, HD), 1)
+    tile = (row // TB) % 4 * 8 + (row // 512) * 4 + (row // 128) % 2
+
+    def fill_onehot(zz, carry):
+        base = (zz // 2) * 32 + (zz % 2) * 2
+        oh[zz] = jnp.where(lane - base == tile, 1.0, 0.0).astype(jnp.bfloat16)
+        return carry
+
+    lax.fori_loop(0, NZ, fill_onehot, 0)
+    mm[...] = jnp.full(mm.shape, MASKED, jnp.float32)
+    ll[...] = jnp.zeros(ll.shape, jnp.float32)
+
+    def clear(i, carry):
+        oo[pl.ds(pl.multiple_of(i * 128, 128), 128), :] = jnp.zeros((128, 2 * HD), jnp.float32)
+        return carry
+
+    lax.fori_loop(0, SLOTS, clear, 0)
+
+    @pl.when(y >= 2)
+    def _():
+        qb[10] = jnp.zeros(qb.shape[1:], qb.dtype)
+        xb[10] = jnp.zeros(xb.shape[1:], xb.dtype)
+
+    @pl.when(last)
+    def _():
+        qb[8:10] = jnp.zeros((2,) + qb.shape[1:], qb.dtype)
+        xb[8:10] = jnp.zeros((2,) + xb.shape[1:], xb.dtype)
+
     pl.semaphore_wait(barrier, NZ + NX * NY - 1)
 
     local(cols(q_ref, z, HZ), zq.at[z], zq_r.at[z])
@@ -85,42 +132,14 @@
         send(ext_ref.at[to], zx.at[z], zx_s.at[s], zx_r.at[z], dev(x, y, to, c))
     for i, ref in enumerate((k_ref, v_ref, w_ref)):
         local(cols(ref, z, HZ), zkv.at[z, i], zk_r.at[z])
-    for s in range(1, NZ):
-        to = (z - OFFS[s] + NZ) % NZ
+
+    def stage_zero(s):
+        to = (z - offset_of(s) + NZ) % NZ
         for i, ref in enumerate((k_ref, v_ref, w_ref)):
             send(cols(ref, to, HZ), zkv.at[z, i], zk_s.at[s], zk_r.at[z], dev(x, y, to, c))
 
-    row = lax.broadcasted_iota(jnp.int32, (CK, HD), 0)
-    lane = lax.broadcasted_iota(jnp.int32, (CK, HD), 1)
-    from_line, inner = (row // 128) % 4, (row // TB) % 4
-    row_x = jnp.where(last, from_line, inner)
-    row_y = jnp.where(last, inner, from_line)
-    tile = row_x * 8 + (row // 512) * 4 + row_y // 2
-
-    def fill_onehot(zz, carry):
-        base = (zz // 2) * 32 + (zz % 2) * 2
-        oh[zz] = jnp.where(lane - base == tile, 1.0, 0.0).astype(jnp.bfloat16)
-        return carry
-
-    lax.fori_loop(0, NZ, fill_onehot, 0)
-    mm[...] = jnp.full(mm.shape, MASKED, jnp.float32)
-    ll[...] = jnp.zeros(ll.shape, jnp.float32)
-
-    def clear(i, carry):
-        oo[pl.ds(pl.multiple_of(i * 128, 128), 128), :] = jnp.zeros((128, 2 * HD), jnp.float32)
-        return carry
-
-    lax.fori_loop(0, SLOTS, clear, 0)
-
-    @pl.when(y >= 2)
-    def _():
-        qb[10] = jnp.zeros(qb.shape[1:], qb.dtype)
-        xb[10] = jnp.zeros(xb.shape[1:], xb.dtype)
-
-    @pl.when(last)
-    def _():
-        qb[8:10] = jnp.zeros((2,) + qb.shape[1:], qb.dtype)
-        xb[8:10] = jnp.zeros((2,) + xb.shape[1:], xb.dtype)
+    for s in range(1, 1 + AHEAD):
+        stage_zero(s)
 
     def spread_queries():
         for i in range(NZ):
@@ -208,107 +227,198 @@
                 j = (x + d) % 4
                 send(zkv.at[zz, :, :, lanes(j)], dst, p1_s.at[s, d], p1_r.at[s, x], dev(j, y, z, c))
 
+        if AHEAD < 7:
+
+            @pl.when(jnp.logical_and(s >= 1, s + AHEAD < NZ))
+            def _():
+                stage_zero(s + AHEAD)
+
+        fifth = zkv.at[zz, :, :, pl.ds(4 * HD, HD)]
+
         @pl.when(last)
         def _():
             to_lines(hk.at[zz, :, block(x), :])
-            local(
-                zkv.at[zz, :, :, pl.ds(4 * HD, HD)], kv.at[zz, :, c, x, pl.ds(3 * TB, TB), :], p1e_r.at[s, 3]
-            )
+            local(fifth, kv.at[zz, :, c, 3, block(x), :], p1e_r.at[s, 3])
 
         @pl.when(jnp.logical_not(last))
         def _():
-            to_lines(kv.at[zz, :, c, y, block(x), :])
-            send(
-                zkv.at[zz, :, :, pl.ds(4 * HD, HD)], kv.at[zz, :, c, x, block(y), :],
-                p1_s.at[s, 0], p1e_r.at[s, y], dev(x, 3, z, c),
-            )
+            to_lines(kv.at[zz, :, c, slot, block(x), :])
+
+        @pl.when(y == 1)
+        def _():
+            send(fifth, kv.at[zz, :, c, 2, block(x), :], p1_s.at[s, 0], p1e_r.at[s, 2], dev(x, 3, z, c))
+
+        @pl.when(even)
+        def _():
+            local(fifth, ek.at[zz, :, block(x), :], p1e_r.at[s, x])
+            for d in range(1, 4):
+                send(
+                    fifth, ek.at[zz, :, block(x), :], p1e_s.at[s, d], p1e_r.at[s, x],
+                    dev((x + d) % 4, y, z, c),
+                )
+
+    low, high = pl.ds(0, 2 * TB), pl.ds(2 * TB, 2 * TB)
 
     def stage_two(s):
         zz = source(s)
         piece = hk.at[zz, :, pl.ds(0, TB), :]
         for i in range(4):
             copy_wait(piece, p1_r.at[s, i])
+        own = kv.at[zz, :, c, slot]
 
         @pl.when(last)
         def _():
-            for t in range(3):
-                send(hk.at[zz], kv.at[zz, :, c, 3], p2_s.at[s, t], p2_r.at[s, 3], dev(x, t, z, c))
+            send(hk.at[zz], own, p2_s.at[s, 0], p2_r.at[s, 3], dev(x, 0, z, c))
+            send(hk.at[zz], own, p2_s.at[s, 1], p2_r.at[s, 3], dev(x, 2, z, c))
+            copy_wait(piece, p1e_r.at[s, 2])
+            copy_wait(piece, p1e_r.at[s, 3])
+            mine = kv.at[zz, :, c, pl.ds(2, 2), block(x), :]
+            for d in range(1, 4):
+                send(mine, mine, e_s.at[s, d], e_r.at[s, x], dev((x + d) % 4, 3, z, c))
+
+        @pl.when(y == 1)
+        def _():
+            send(own, own, p2_s.at[s, 0], p2_r.at[s, slot], dev(x, 0, z, c))
+            send(own, own, p2_s.at[s, 1], p2_r.at[s, slot], dev(x, 2, z, c))
+
+        @pl.when(even)
+        def _():
+            send(own, own, p2_s.at[s, 0], p2_r.at[s, slot], dev(x, 1, z, c))
+            send(
+                kv.at[zz, :, c, slot, high, :], fk.at[zz, slot], p2_s.at[s, 1], f_r.at[s, slot],
+                dev(x, 3, z, c),
+            )
             for i in range(4):
                 copy_wait(piece, p1e_r.at[s, i])
-            own = kv.at[zz, :, c, x]
-            for d in range(1, 4):
-                send(own, own, p2e_s.at[s, d], p2_r.at[s, x], dev((x + d) % 4, y, z, c))
-
-        @pl.when(jnp.logical_not(last))
-        def _():
-            own = kv.at[zz, :, c, y]
-            for d in range(1, 3):
-                send(own, own, p2_s.at[s, d], p2_r.at[s, y], dev(x, (y + d) % 3, z, c))
+            send(ek.at[zz], own, e_s.at[s, 0], p2_r.at[s, slot], dev(x, 3, z, c))
+
+    def stage_relay(s):
+        zz = source(s)
+
+        def part(who, rows):
+            return kv.at[zz, :, c, who, rows, :]
+
+        @pl.when(last)
+        def _():
+            for i in range(2):
+                copy_wait(fk.at[zz, i], f_r.at[s, i])
+                send(fk.at[zz, i], part(i, high), p3_s.at[s, i], h_r.at[s, 1], dev(x, 2 - 2 * i, z, c))
+
+        @pl.when(y == 1)
+        def _():
+            for i in range(2):
+                copy_wait(hk.at[zz], p2_r.at[s, i])
+                send(part(i, low), part(i, low), p3_s.at[s, i], h_r.at[s, 0], dev(x, 2 - 2 * i, z, c))
+
+        @pl.when(y == 0)
+        def _():
+            copy_wait(hk.at[zz], p2_r.at[s, 2])
+            copy_wait(hk.at[zz], p2_r.at[s, 3])
+            send(part(3, low), part(3, low), p3_s.at[s, 0], h_r.at[s, 0], dev(x, 1, z, c))
+
+        @pl.when(y == 2)
+        def _():
+            copy_wait(hk.at[zz], p2_r.at[s, 2])
+            copy_wait(hk.at[zz], p2_r.at[s, 3])
+            send(part(3, high), part(3, high), p3_s.at[s, 0], h_r.at[s, 1], dev(x, 1, z, c))
 
     def stage_three(s):
         zz = source(s)
-        own = jnp.where(last, x, y)
-        for d in range(1, 4):
-            copy_wait(hk.at[zz], p2_r.at[s, (own + d) % 4])
+
+        @pl.when(last)
+        def _():
+            for i in range(2):
+                copy_wait(hk.at[zz], p2_r.at[s, i])
+            for d in range(1, 4):
+                copy_wait(kv.at[zz, :, 0, pl.ds(2, 2), pl.ds(0, TB), :], e_r.at[s, (x + d) % 4])
+
+        @pl.when(jnp.logical_not(last))
+        def _():
+            for i in range(2):
+                copy_wait(fk.at[zz, 0], h_r.at[s, i])
+
         half = kv.at[zz, :, c]
         send(half, half, c_s.at[s], c_r.at[s], dev(x, y, z, 1 - c))
 
     scale = HD ** (-0.5) * LOG2E
+
+    def fold(parts, op):
+        while len(parts) > 1:
+            parts = [
+                op(parts[i], parts[i + 1]) if i + 1 < len(parts) else parts[i]
+                for i in range(0, len(parts), 2)
+            ]
+        return parts[0]
 
     def attend(s):
         zz = source(s)
         copy_wait(kv.at[zz, :, 0], c_r.at[s])
 
-        def some_rows(i, carry):
-            rows = pl.ds(pl.multiple_of(i * QC, 32), QC)
-            keys = jnp.concatenate([kv[zz, 0].reshape(CK, HD), oh[zz]], axis=1)
+        def score(i):
+            rows = pl.ds(i * QC, QC)
+            tiles = []
+            for k in range(0, CK, 256):
+                keys = jnp.concatenate(
+                    [kv[zz, 0].reshape(CK, HD)[k : k + 256], oh[zz, k : k + 256]], axis=1
+                )
+                scores = lax.dot_general(
+                    qa[rows, :], keys, (((1,), (1,)), ((), ())), preferred_element_type=jnp.float32
+                )
+                tiles += [scores[:, :128], scores[:, 128:]]
+            return tiles, jnp.max(fold(tiles, jnp.maximum), axis=1, keepdims=True)
+
+        def gather(i, tiles, largest):
+            rows = pl.ds(i * QC, QC)
+            old = mm[rows, :]
+            new = jnp.maximum(old, largest)
+            weights = [jnp.exp2((t - new) * scale) for t in tiles]
+            shrink = jnp.exp2((old - new) * scale)
+            mm[rows, :] = new
+            ll[rows, :] = ll[rows, :] * shrink + fold(weights, jnp.add)
             values = jnp.concatenate([kv[zz, 1].reshape(CK, HD), kv[zz, 2].reshape(CK, HD)], axis=1)
-            scores = lax.dot_general(
-                qa[rows, :], keys, (((1,), (1,)), ((), ())), preferred_element_type=jnp.float32
-            )
-            old = mm[rows, :]
-            new = jnp.maximum(old, jnp.max(scores, axis=1, keepdims=True))
-            weights = jnp.exp2((scores - new[:, 0:1]) * scale)
-            shrink = jnp.exp2((old - new) * scale)
-            part = weights[:, 0:128]
-            for t in range(1, CK // 128):
-                part = part + weights[:, t * 128 : (t + 1) * 128]
-            mm[rows, :] = new
-            ll[rows, :] = ll[rows, :] * shrink + part
-            sums = jnp.dot(weights.astype(jnp.bfloat16), values, preferred_element_type=jnp.float32)
+            low_weights = jnp.concatenate([w.astype(jnp.bfloat16) for w in weights], axis=1)
+            sums = jnp.dot(low_weights, values, preferred_element_type=jnp.float32)
             oo[rows, :] = oo[rows, :] * jnp.concatenate([shrink, shrink], axis=1) + sums
-            return carry
-
-        lax.fori_loop(0, ROWS // QC, some_rows, 0)
-
-    spread_queries()
-    stage_one(0)
-    lend_queries()
-    stage_one(1)
-    stage_two(0)
-    ready_queries()
-    stage_one(2)
-    stage_two(1)
-    stage_three(0)
+
+        held = None
+        for i in range(ROWS // QC):
+            now = score(i)
+            if held is not None:
+                gather(i - 1, *held)
+            held = now
+        gather(ROWS // QC - 1, *held)
+
+    def moves(t):
+        for stage, lag in zip((stage_three, stage_relay, stage_two, stage_one), LAGS[::-1]):
+
+            @pl.when(jnp.logical_and(t >= lag, t < NZ + lag))
+            def _(stage=stage, lag=lag):
+                stage(t - lag)
+
+    def fill(t, carry):
+        moves(t)
+
+        @pl.when(t == 0)
+        def _():
+            spread_queries()
+
+        @pl.when(t == 1)
+        def _():
+            lend_queries()
+
+        @pl.when(t == 2)
+        def _():
+            ready_queries()
+
+        return carry
 
     def step(t, carry):
-        attend(t)
-
-        @pl.when(t + 3 < NZ)
-        def _():
-            stage_one(t + 3)
-
-        @pl.when(t + 2 < NZ)
-        def _():
-            stage_two(t + 2)
-
-        @pl.when(t + 1 < NZ)
-        def _():
-            stage_three(t + 1)
-
+        attend(t - READY)
+        moves(t)
         return carry
 
-    lax.fori_loop(0, NZ, step, 0)
+    lax.fori_loop(0, READY, fill, 0)
+    lax.fori_loop(READY, READY + NZ, step, 0)
 
     def finish(i, carry):
         rows = pl.ds(pl.multiple_of(i * 128, 128), 128)
@@ -377,17 +487,29 @@
             wait_send(hk.at[0, :, pl.ds(0, TB), :], p1_s.at[s, d])
         wait_send(kv.at[0, :, 0], c_s.at[s])
 
+        wait_send(hk.at[0], p2_s.at[s, 0])
+        wait_send(fk.at[0, 0], p3_s.at[s, 0])
+
         @pl.when(last)
         def _():
-            for t in range(3):
-                wait_send(hk.at[0], p2_s.at[s, t])
-                wait_send(hk.at[0], p2e_s.at[s, t + 1])
-
-        @pl.when(jnp.logical_not(last))
+            for d in range(1, 4):
+                wait_send(kv.at[0, :, 0, pl.ds(2, 2), pl.ds(0, TB), :], e_s.at[s, d])
+
+        @pl.when(jnp.logical_not(even))
+        def _():
+            wait_send(hk.at[0], p2_s.at[s, 1])
+            wait_send(fk.at[0, 0], p3_s.at[s, 1])
+
+        @pl.when(y == 1)
         def _():
             wait_send(hk.at[0, :, pl.ds(0, TB), :], p1_s.at[s, 0])
-            for d in range(1, 3):
-                wait_send(hk.at[0], p2_s.at[s, d])
+
+        @pl.when(even)
+        def _():
+            wait_send(fk.at[0, 0], p2_s.at[s, 1])
+            wait_send(hk.at[0], e_s.at[s, 0])
+            for d in range(1, 4):
+                wait_send(hk.at[0, :, pl.ds(0, TB), :], p1e_s.at[s, d])
 
         return carry
 
@@ -425,18 +547,6 @@
 
 
 def on_device(query_src, key_src, value_src, value_edit, tile_mask, word_map, blend_table):
-    words, heads = blend_table.shape
-    half = lax.axis_index("head") // 2
-    mask_row = lax.dynamic_index_in_dim(tile_mask, half, 0, keepdims=False)
-    bias = jnp.where(mask_row == 1, 0.0, MASKED).astype(jnp.float32)
-    onehot = (jnp.arange(words, dtype=jnp.int32)[:, None] == word_map[None, :]).astype(jnp.float32)
-    shares = lax.dot_general(
-        blend_table, onehot, (((0,), (0,)), ((), ())), precision=lax.Precision.HIGHEST
-    )
-    shares = jnp.pad(shares.reshape(NZ, HZ, TB), ((0, 0), (0, 0), (0, 128 - TB)))
-    ext = jnp.concatenate(
-        [jnp.broadcast_to(bias, (NZ, 1, 128)), shares, jnp.zeros((NZ, 2, 128), jnp.float32)], axis=1
-    )
     bf, f32 = jnp.bfloat16, jnp.float32
     dma = pltpu.SemaphoreType.DMA
     anywhere = pl.BlockSpec(memory_space=pl.ANY)
@@ -444,15 +554,18 @@
     return pl.pallas_call(
         body,
         out_shape=jax.ShapeDtypeStruct(query_src.shape, bf),
-        in_specs=[anywhere] * 4 + [vmem],
-        out_specs=anywhere,
+        in_specs=[anywhere] * 4 + [vmem] * 3,
+        out_specs=vmem,
         scratch_shapes=[
+            pltpu.VMEM((NZ, 8, 128), f32),
             pltpu.VMEM((NZ, TB, HZ * HD), bf),
             pltpu.VMEM((NZ, 8, 128), f32),
             pltpu.VMEM((NZ, 3, TB, HZ * HD), bf),
             pltpu.VMEM((NZ, 128, HD), bf),
             pltpu.VMEM((NZ, 4, 8, 128), f32),
             pltpu.VMEM((NZ, 3, 128, HD), bf),
+            pltpu.VMEM((NZ, 3, 128, HD), bf),
+            pltpu.VMEM((NZ, 2, 3, 2 * TB, HD), bf),
             pltpu.VMEM((SLOTS, 128, HD), bf),
             pltpu.VMEM((SLOTS, 4, 8, 128), f32),
             pltpu.VMEM((NZ, 3, NC, 4, 128, HD), bf),
@@ -468,17 +581,18 @@
             dma((4,)), dma((4,)), dma((4,)), dma((4,)), dma((4,)), dma((4,)),
             dma((3,)), dma(()), dma((3,)), dma(()),
             dma((NZ, 4)), dma((NZ, 4)), dma((NZ, 4)),
-            dma((NZ, 3)), dma((NZ, 4)), dma((NZ, 4)), dma((NZ,)), dma((NZ,)),
+            dma((NZ, 4)), dma((NZ, 2)), dma((NZ, 4)), dma((NZ, 4)), dma((NZ, 4)),
+            dma((NZ, 2)), dma((NZ, 2)), dma((NZ, 2)), dma((NZ,)), dma((NZ,)),
             dma((4,)), dma((4,)), dma((4,)), dma((4, 3)), dma((1,)), dma(()),
             dma((NZ,)), dma((NZ,)),
         ],
         compiler_params=pltpu.CompilerParams(
-            collective_id=0, has_side_effects=True, vmem_limit_bytes=48 * 1024 * 1024
+            collective_id=0, has_side_effects=True, vmem_limit_bytes=VMEM_LIMIT
         ),
         cost_estimate=pl.CostEstimate(
             flops=4 * ROWS * 8192 * 256, bytes_accessed=8 * 1024 * 1024, transcendentals=ROWS * 8192
         ),
-    )(query_src, key_src, value_src, value_edit, ext)
+    )(query_src, key_src, value_src, value_edit, tile_mask, word_map.reshape(1, TB), blend_table.T)
 
 
 def solution(mesh):

time: 117 us -> 88.5 us (0.76); the launches traced: 116 us -> 88.3 us
  Pallas kernels: 109 us -> 86.6 us
  local copies, waits for them, and re-layouts: 5.46 us -> 1.72 us
    pallas_call x1, Pallas kernels: 109 us -> 86.6 us  [on_device(): pl.pallas_call(body, out_shape=jax.ShapeDtypeStruct(query_src.shape, bf),...]
    unnamed x13 -> x1, local copies, waits for them, and re-layouts: 5.28 us -> 1.72 us
where the time goes in v2:
time: 88.5 us; the launch traced here: 88.3 us
  Pallas kernels  86.6 us (98%)
  local copies, waits for them, and re-layouts  1.72 us (2%)
    pallas_call x1, Pallas kernels, on_device(): pl.pallas_call(body, out_shape=jax.ShapeDtypeStruct(query_src.shape, bf),...  86.6 us

profile of v2, /device:TPU:56, one launch (start us, length us, event | category | flops | bytes accessed | tf_op | source)
XLA Modules:
  0.0 88.3 jit_solution(7176951067890312039)
XLA Ops:
  0.0 86.6 %shard_map.73 = bf16[32,5120]{1,0:T(8,128)(2,1)} custom-call(bf16[32,5120]{1,0:T(8,128)(2,1)} %q_ref.1, bf16[32,5120]{1,0:T(8,128)(2,1)} %k_ref.1, bf16[32,5120]{1,0:T(8,128)(2,1)} %v_ref.1, bf16[32,5120]{1,0:T(8,128)(2,1)} %w_ref.1, s32[4,128]{1,0:T(4,128)} %mask_ref.1, s32[1,32]{1,0:T(1,128)} %bitcast.3, f32[40,512]{1,0:T(8,128)} %bitcast.2), custom_call_target="tpu_custom_call" | custom-call | flops 11811160064 | bytes 8388608 | tf_op jit(solution)/shard_map/pallas_call | solution.py:554
  86.6 1.7 %copy.9 = bf16[32,5120]{1,0:T(8,128)(2,1)} copy(bf16[32,5120]{1,0:T(8,128)(2,1)} %shard_map.73) | data formatting | bytes 655360

commit v3 on v2

--- a/solution.py
+++ b/solution.py
@@ -17,8 +17,7 @@
 MASKED = -(2.0**100)
 OFFS = (0, 1, -1, 2, -2, 3, -3, 4)
 VMEM_LIMIT = 60 * 1024 * 1024
-LAGS = (0, 2, 4, 6)
-READY = 8
+LEADS = (1, 3, 5)
 AHEAD = 7
 LOG2E = 1.4426950408889634
 
@@ -34,11 +33,11 @@
 
 def body(
     q_ref, k_ref, v_ref, w_ref, mask_ref, word_ref, blend_ref, out_ref,
-    ext_ref, zq, zx, zkv, hq, hx, hk, ek, fk, qb, xb, kv, oh, qa, mix, mm, ll, oo, ro, ox,
+    ext_ref, zq, zx, zkv, hq, hx, hk, ek, qb, xb, kv, oh, qa, mix, mm, ll, oo, ro, ox,
     zq_s, zq_r, zx_s, zx_r, zk_s, zk_r,
     pq_s, pq_r, pqe_r, px_s, px_r, pxe_r, bq_s, bq_r, bx_s, bx_r,
-    p1_s, p1_r, p1e_r, p1e_s, p2_s, p2_r, e_s, e_r, f_r, p3_s, h_r, c_s, c_r,
-    r1_s, r1_r, rb_s, rb_r, re_s, re_r, r2_s, r2_r,
+    p1_s, p1_r, p1e_r, p1e_s, p2_s, p2_r, e_s, e_r, c_s, c_r,
+    r1_s, r1_r, rb_s, rb_r, re_r, r2_s, r2_r,
 ):
     seq = lax.axis_index("seq")
     head = lax.axis_index("head")
@@ -134,7 +133,7 @@
         local(cols(ref, z, HZ), zkv.at[z, i], zk_r.at[z])
 
     def stage_zero(s):
-        to = (z - offset_of(s) + NZ) % NZ
+        to = (z - (OFFS[s] if isinstance(s, int) else offset_of(s)) + NZ) % NZ
         for i, ref in enumerate((k_ref, v_ref, w_ref)):
             send(cols(ref, to, HZ), zkv.at[z, i], zk_s.at[s], zk_r.at[z], dev(x, y, to, c))
 
@@ -215,7 +214,7 @@
         lax.fori_loop(0, SLOTS, one, 0)
 
     def source(s):
-        return (z + offset_of(s) + NZ) % NZ
+        return (z + (OFFS[s] if isinstance(s, int) else offset_of(s)) + NZ) % NZ
 
     def stage_one(s):
         zz = source(s)
@@ -256,8 +255,6 @@
                     fifth, ek.at[zz, :, block(x), :], p1e_s.at[s, d], p1e_r.at[s, x],
                     dev((x + d) % 4, y, z, c),
                 )
-
-    low, high = pl.ds(0, 2 * TB), pl.ds(2 * TB, 2 * TB)
 
     def stage_two(s):
         zz = source(s)
@@ -270,6 +267,7 @@
         def _():
             send(hk.at[zz], own, p2_s.at[s, 0], p2_r.at[s, 3], dev(x, 0, z, c))
             send(hk.at[zz], own, p2_s.at[s, 1], p2_r.at[s, 3], dev(x, 2, z, c))
+            send(hk.at[zz], own, p2_s.at[s, 2], p2_r.at[s, 3], dev(x, 1, z, c))
             copy_wait(piece, p1e_r.at[s, 2])
             copy_wait(piece, p1e_r.at[s, 3])
             mine = kv.at[zz, :, c, pl.ds(2, 2), block(x), :]
@@ -284,58 +282,25 @@
         @pl.when(even)
         def _():
             send(own, own, p2_s.at[s, 0], p2_r.at[s, slot], dev(x, 1, z, c))
-            send(
-                kv.at[zz, :, c, slot, high, :], fk.at[zz, slot], p2_s.at[s, 1], f_r.at[s, slot],
-                dev(x, 3, z, c),
-            )
+            send(own, own, p2_s.at[s, 1], p2_r.at[s, slot], dev(x, 2 - y, z, c))
             for i in range(4):
                 copy_wait(piece, p1e_r.at[s, i])
             send(ek.at[zz], own, e_s.at[s, 0], p2_r.at[s, slot], dev(x, 3, z, c))
 
-    def stage_relay(s):
+    def stage_three(s):
         zz = source(s)
 
-        def part(who, rows):
-            return kv.at[zz, :, c, who, rows, :]
-
         @pl.when(last)
-        def _():
-            for i in range(2):
-                copy_wait(fk.at[zz, i], f_r.at[s, i])
-                send(fk.at[zz, i], part(i, high), p3_s.at[s, i], h_r.at[s, 1], dev(x, 2 - 2 * i, z, c))
-
-        @pl.when(y == 1)
         def _():
             for i in range(2):
                 copy_wait(hk.at[zz], p2_r.at[s, i])
-                send(part(i, low), part(i, low), p3_s.at[s, i], h_r.at[s, 0], dev(x, 2 - 2 * i, z, c))
-
-        @pl.when(y == 0)
-        def _():
-            copy_wait(hk.at[zz], p2_r.at[s, 2])
-            copy_wait(hk.at[zz], p2_r.at[s, 3])
-            send(part(3, low), part(3, low), p3_s.at[s, 0], h_r.at[s, 0], dev(x, 1, z, c))
-
-        @pl.when(y == 2)
-        def _():
-            copy_wait(hk.at[zz], p2_r.at[s, 2])
-            copy_wait(hk.at[zz], p2_r.at[s, 3])
-            send(part(3, high), part(3, high), p3_s.at[s, 0], h_r.at[s, 1], dev(x, 1, z, c))
-
-    def stage_three(s):
-        zz = source(s)
-
-        @pl.when(last)
-        def _():
-            for i in range(2):
-                copy_wait(hk.at[zz], p2_r.at[s, i])
             for d in range(1, 4):
                 copy_wait(kv.at[zz, :, 0, pl.ds(2, 2), pl.ds(0, TB), :], e_r.at[s, (x + d) % 4])
 
         @pl.when(jnp.logical_not(last))
         def _():
-            for i in range(2):
-                copy_wait(fk.at[zz, 0], h_r.at[s, i])
+            for d in range(1, 4):
+                copy_wait(hk.at[zz], p2_r.at[s, (slot + d) % 4])
 
         half = kv.at[zz, :, c]
         send(half, half, c_s.at[s], c_r.at[s], dev(x, y, z, 1 - c))
@@ -388,91 +353,122 @@
             held = now
         gather(ROWS // QC - 1, *held)
 
-    def moves(t):
-        for stage, lag in zip((stage_three, stage_relay, stage_two, stage_one), LAGS[::-1]):
-
-            @pl.when(jnp.logical_and(t >= lag, t < NZ + lag))
-            def _(stage=stage, lag=lag):
-                stage(t - lag)
-
-    def fill(t, carry):
-        moves(t)
-
-        @pl.when(t == 0)
-        def _():
-            spread_queries()
-
-        @pl.when(t == 1)
-        def _():
-            lend_queries()
-
-        @pl.when(t == 2)
-        def _():
-            ready_queries()
+    def step(t, carry):
+        attend(t)
+        for stage, lead in zip((stage_three, stage_two, stage_one), LEADS):
+
+            @pl.when(t + lead < NZ)
+            def _(stage=stage, lead=lead):
+                stage(t + lead)
 
         return carry
 
-    def step(t, carry):
-        attend(t - READY)
-        moves(t)
-        return carry
-
-    lax.fori_loop(0, READY, fill, 0)
-    lax.fori_loop(READY, READY + NZ, step, 0)
-
-    def finish(i, carry):
+    stage_one(0)
+    stage_two(0)
+    stage_three(0)
+    spread_queries()
+    stage_one(1)
+    stage_one(2)
+    lend_queries()
+    stage_two(1)
+    stage_two(2)
+    stage_one(3)
+    ready_queries()
+    for s in range(4, LEADS[2]):
+        stage_one(s)
+    for s in range(3, LEADS[1]):
+        stage_two(s)
+    lax.fori_loop(0, NZ, step, 0)
+
+    def finish(i):
         rows = pl.ds(pl.multiple_of(i * 128, 128), 128)
         total = jnp.sum(ll[rows, :], axis=1, keepdims=True)
         share = mix[rows, :]
         both = oo[rows, :] / total
         ro[i] = (share * both[:, HD:] + (1.0 - share) * both[:, :HD]).astype(jnp.bfloat16)
-        return carry
-
-    lax.fori_loop(0, SLOTS, finish, 0)
+
+    e_lanes = pl.ds(4 * HD, HD)
+
+    far, near = 4 - 4 * (z // 4), 4 * (z // 4)
+
+    def finish_some(first, count):
+        def one(i, carry):
+            finish(first + i)
+            return carry
+
+        lax.fori_loop(0, count, one, 0)
+
+    def return_lent(n):
+        for j in range(4):
+            send(
+                ro.at[pl.ds(8, n), pl.ds(j * TB, TB), :], ox.at[pl.ds(3 * y, n), :, lanes(x)],
+                rb_s.at[j], rb_r.at[y, x], dev(j, 3, z, c),
+            )
+
+    def return_own(first, h):
+        finish_some(first, 4)
+        slots, which = pl.ds(first, 4), first // 4
+
+        @pl.when(last)
+        def _():
+            local(ro.at[slots, pl.ds(3 * TB, TB), :], ox.at[slots, :, e_lanes], re_r.at[which])
+            for t in range(3):
+                send(
+                    ro.at[slots, pl.ds(t * TB, TB), :], ox.at[slots, :, e_lanes],
+                    r1_s.at[h, t], re_r.at[which], dev(x, t, z, c),
+                )
+
+        @pl.when(jnp.logical_not(last))
+        def _():
+            mine = lanes(x)
+            local(ro.at[slots, block(x), :], ox.at[slots, :, mine], r1_r.at[which, x])
+            for d in range(1, 4):
+                j = (x + d) % 4
+                send(
+                    ro.at[slots, block(j), :], ox.at[slots, :, mine],
+                    r1_s.at[h, d - 1], r1_r.at[which, x], dev(j, y, z, c),
+                )
+
+    finish_some(8, 3)
+
+    @pl.when(y < 2)
+    def _():
+        return_lent(3)
+
+    @pl.when(y == 2)
+    def _():
+        return_lent(2)
+
+    return_own(far, 0)
+    return_own(near, 1)
+    target = cols(out_ref, z, HZ)
 
     @pl.when(last)
     def _():
-        e_lanes = pl.ds(4 * HD, HD)
-        local(ro.at[pl.ds(0, 8), pl.ds(3 * TB, TB), :], ox.at[:, :, e_lanes], re_r)
         for t in range(3):
-            send(ro.at[pl.ds(0, 8), pl.ds(t * TB, TB), :], ox.at[:, :, e_lanes], r1_s.at[t], re_r, dev(x, t, z, c))
-        for j in range(4):
-            for t in range(3):
-                n = 3 if t < 2 else 2
-                copy_wait(ox.at[pl.ds(3 * t, n), :, lanes(j)], rb_r.at[j, t])
-
-    @pl.when(jnp.logical_not(last))
-    def _():
-        mine = lanes(x)
-        local(ro.at[pl.ds(0, 8), block(x), :], ox.at[:, :, mine], r1_r.at[x])
-        for d in range(1, 4):
-            j = (x + d) % 4
-            send(ro.at[pl.ds(0, 8), block(j), :], ox.at[:, :, mine], r1_s.at[d], r1_r.at[x], dev(j, y, z, c))
-        for i in range(4):
-
-            @pl.when(y < 2)
-            def _():
-                send(
-                    ro.at[pl.ds(8, 3), pl.ds(i * TB, TB), :], ox.at[pl.ds(3 * y, 3), :, mine],
-                    rb_s.at[i], rb_r.at[x, y], dev(i, 3, z, c),
-                )
-
-            @pl.when(y == 2)
-            def _():
-                send(
-                    ro.at[pl.ds(8, 2), pl.ds(i * TB, TB), :], ox.at[pl.ds(6, 2), :, mine],
-                    rb_s.at[i], rb_r.at[x, 2], dev(i, 3, z, c),
-                )
-
-        for i in range(4):
-            copy_wait(ox.at[:, :, lanes(i)], r1_r.at[i])
-
-    copy_wait(ox.at[:, :, pl.ds(4 * HD, HD)], re_r)
-    target = cols(out_ref, z, HZ)
+            n = 3 if t < 2 else 2
+            for i in range(4):
+                copy_wait(ox.at[pl.ds(3 * t, n), :, lanes(i)], rb_r.at[t, i])
+
+    def arrived(first):
+        slots, which = pl.ds(first, 4), first // 4
+
+        @pl.when(jnp.logical_not(last))
+        def _():
+            for i in range(4):
+                copy_wait(ox.at[slots, :, lanes(i)], r1_r.at[which, i])
+
+        copy_wait(ox.at[slots, :, e_lanes], re_r.at[which])
+
+    arrived(far)
+    for i in range(4):
+        zz = far + (z + i) % 4
+        send(ox.at[zz], target, r2_s.at[i], r2_r.at[z], dev(x, y, zz, c))
+    arrived(near)
+    for i in range(1, 4):
+        zz = near + (z + i) % 4
+        send(ox.at[zz], target, r2_s.at[3 + i], r2_r.at[z], dev(x, y, zz, c))
     local(ox.at[z], target, r2_r.at[z])
-    for s in range(1, NZ):
-        to = (z - OFFS[s] + NZ) % NZ
-        send(ox.at[to], target, r2_s.at[s], r2_r.at[z], dev(x, y, to, c))
 
     for s in range(1, NZ):
         wait_send(zq.at[0], zq_s.at[s])
@@ -488,17 +484,16 @@
         wait_send(kv.at[0, :, 0], c_s.at[s])
 
         wait_send(hk.at[0], p2_s.at[s, 0])
-        wait_send(fk.at[0, 0], p3_s.at[s, 0])
 
         @pl.when(last)
         def _():
             for d in range(1, 4):
                 wait_send(kv.at[0, :, 0, pl.ds(2, 2), pl.ds(0, TB), :], e_s.at[s, d])
+            wait_send(hk.at[0], p2_s.at[s, 2])
 
         @pl.when(jnp.logical_not(even))
         def _():
             wait_send(hk.at[0], p2_s.at[s, 1])
-            wait_send(fk.at[0, 0], p3_s.at[s, 1])
 
         @pl.when(y == 1)
         def _():
@@ -506,7 +501,7 @@
 
         @pl.when(even)
         def _():
-            wait_send(fk.at[0, 0], p2_s.at[s, 1])
+            wait_send(hk.at[0], p2_s.at[s, 1])
             wait_send(hk.at[0], e_s.at[s, 0])
             for d in range(1, 4):
                 wait_send(hk.at[0, :, pl.ds(0, TB), :], p1e_s.at[s, d])
@@ -521,27 +516,27 @@
             n = 3 if t < 2 else 2
             wait_send(hq.at[pl.ds(0, n)], bq_s.at[t])
             wait_send(hx.at[pl.ds(0, n)], bx_s.at[t])
-            wait_send(hq.at[:, pl.ds(0, TB), :], r1_s.at[t])
 
     @pl.when(jnp.logical_not(last))
     def _():
         wait_send(hq.at[:, pl.ds(0, TB), :], pq_s.at[0])
         wait_send(zx, px_s.at[0])
-        for d in range(1, 4):
-            wait_send(hq.at[:, pl.ds(0, TB), :], r1_s.at[d])
 
         @pl.when(y < 2)
         def _():
-            for i in range(4):
-                wait_send(hq.at[pl.ds(0, 3), pl.ds(0, TB), :], rb_s.at[i])
+            for j in range(4):
+                wait_send(ro.at[pl.ds(0, 3), pl.ds(0, TB), :], rb_s.at[j])
 
         @pl.when(y == 2)
         def _():
-            for i in range(4):
-                wait_send(hq.at[pl.ds(0, 2), pl.ds(0, TB), :], rb_s.at[i])
-
-    for s in range(1, NZ):
-        wait_send(ox.at[0], r2_s.at[s])
+            for j in range(4):
+                wait_send(ro.at[pl.ds(0, 2), pl.ds(0, TB), :], rb_s.at[j])
+
+    for h in range(2):
+        for t in range(3):
+            wait_send(ro.at[pl.ds(0, 4), pl.ds(0, TB), :], r1_s.at[h, t])
+    for i in range(NZ - 1):
+        wait_send(ox.at[0], r2_s.at[i])
     for i in range(NZ):
         copy_wait(ox.at[0], r2_r.at[i])
 
@@ -565,7 +560,6 @@
             pltpu.VMEM((NZ, 4, 8, 128), f32),
             pltpu.VMEM((NZ, 3, 128, HD), bf),
             pltpu.VMEM((NZ, 3, 128, HD), bf),
-            pltpu.VMEM((NZ, 2, 3, 2 * TB, HD), bf),
             pltpu.VMEM((SLOTS, 128, HD), bf),
             pltpu.VMEM((SLOTS, 4, 8, 128), f32),
             pltpu.VMEM((NZ, 3, NC, 4, 128, HD), bf),
@@ -581,9 +575,8 @@
             dma((4,)), dma((4,)), dma((4,)), dma((4,)), dma((4,)), dma((4,)),
             dma((3,)), dma(()), dma((3,)), dma(()),
             dma((NZ, 4)), dma((NZ, 4)), dma((NZ, 4)),
-            dma((NZ, 4)), dma((NZ, 2)), dma((NZ, 4)), dma((NZ, 4)), dma((NZ, 4)),
-            dma((NZ, 2)), dma((NZ, 2)), dma((NZ, 2)), dma((NZ,)), dma((NZ,)),
-            dma((4,)), dma((4,)), dma((4,)), dma((4, 3)), dma((1,)), dma(()),
+            dma((NZ, 4)), dma((NZ, 3)), dma((NZ, 4)), dma((NZ, 4)), dma((NZ, 4)), dma((NZ,)), dma((NZ,)),
+            dma((2, 3)), dma((2, 4)), dma((4,)), dma((3, 4)), dma((2,)),
             dma((NZ,)), dma((NZ,)),
         ],
         compiler_params=pltpu.CompilerParams(

time: 88.5 us -> 85.7 us (0.968)
  Pallas kernels: 86.6 us -> 83.5 us
    pallas_call x1, Pallas kernels: 86.6 us -> 83.5 us  [on_device(): pl.pallas_call(body, out_shape=jax.ShapeDtypeStruct(query_src.shape, bf),...]
where the time goes in v3:
time: 85.7 us; the launch traced here: 85.2 us
  Pallas kernels  83.5 us (97%)
  local copies, waits for them, and re-layouts  1.72 us (2%)
    pallas_call x1, Pallas kernels, on_device(): pl.pallas_call(body, out_shape=jax.ShapeDtypeStruct(query_src.shape, bf),...  83.5 us
    unnamed x1, local copies, waits for them, and re-layouts  1.72 us

profile of v3, /device:TPU:56, one launch (start us, length us, event | category | flops | bytes accessed | tf_op | source)
XLA Modules:
  0.0 85.2 jit_solution(8188082646763101265)
XLA Ops:
  0.0 83.5 %shard_map.73 = bf16[32,5120]{1,0:T(8,128)(2,1)} custom-call(bf16[32,5120]{1,0:T(8,128)(2,1)} %q_ref.1, bf16[32,5120]{1,0:T(8,128)(2,1)} %k_ref.1, bf16[32,5120]{1,0:T(8,128)(2,1)} %v_ref.1, bf16[32,5120]{1,0:T(8,128)(2,1)} %w_ref.1, s32[4,128]{1,0:T(4,128)} %mask_ref.1, s32[1,32]{1,0:T(1,128)} %bitcast.3, f32[40,512]{1,0:T(8,128)} %bitcast.2), custom_call_target="tpu_custom_call" | custom-call | flops 11811160064 | bytes 8388608 | tf_op jit(solution)/shard_map/pallas_call | solution.py:549
  83.5 1.7 %copy.9 = bf16[32,5120]{1,0:T(8,128)(2,1)} copy(bf16[32,5120]{1,0:T(8,128)(2,1)} %shard_map.73) | data formatting | bytes 655360

commit v4 on v3

--- a/solution.py
+++ b/solution.py
@@ -17,7 +17,7 @@
 MASKED = -(2.0**100)
 OFFS = (0, 1, -1, 2, -2, 3, -3, 4)
 VMEM_LIMIT = 60 * 1024 * 1024
-LEADS = (1, 3, 5)
+LEADS = (2, 4, 6)
 AHEAD = 7
 LOG2E = 1.4426950408889634
 
@@ -378,6 +378,8 @@
         stage_one(s)
     for s in range(3, LEADS[1]):
         stage_two(s)
+    for s in range(1, LEADS[0]):
+        stage_three(s)
     lax.fori_loop(0, NZ, step, 0)
 
     def finish(i):

time: 85.7 us -> 83.6 us (0.975)
  Pallas kernels: 83.5 us -> 81.1 us
    pallas_call x1, Pallas kernels: 83.5 us -> 81.1 us  [on_device(): pl.pallas_call(body, out_shape=jax.ShapeDtypeStruct(query_src.shape, bf),...]
where the time goes in v4:
time: 83.6 us; the launch traced here: 82.8 us
  Pallas kernels  81.1 us (97%)
  local copies, waits for them, and re-layouts  1.72 us (2%)
    pallas_call x1, Pallas kernels, on_device(): pl.pallas_call(body, out_shape=jax.ShapeDtypeStruct(query_src.shape, bf),...  81.1 us
    unnamed x1, local copies, waits for them, and re-layouts  1.72 us

profile of v4, /device:TPU:56, one launch (start us, length us, event | category | flops | bytes accessed | tf_op | source)
XLA Modules:
  0.0 82.8 jit_solution(6961378743955841943)
XLA Ops:
  0.0 81.1 %shard_map.73 = bf16[32,5120]{1,0:T(8,128)(2,1)} custom-call(bf16[32,5120]{1,0:T(8,128)(2,1)} %q_ref.1, bf16[32,5120]{1,0:T(8,128)(2,1)} %k_ref.1, bf16[32,5120]{1,0:T(8,128)(2,1)} %v_ref.1, bf16[32,5120]{1,0:T(8,128)(2,1)} %w_ref.1, s32[4,128]{1,0:T(4,128)} %mask_ref.1, s32[1,32]{1,0:T(1,128)} %bitcast.3, f32[40,512]{1,0:T(8,128)} %bitcast.2), custom_call_target="tpu_custom_call" | custom-call | flops 11811160064 | bytes 8388608 | tf_op jit(solution)/shard_map/pallas_call | solution.py:551
  81.1 1.7 %copy.9 = bf16[32,5120]{1,0:T(8,128)(2,1)} copy(bf16[32,5120]{1,0:T(8,128)(2,1)} %shard_map.73) | data formatting | bytes 655360
